TPU v7x, 128 devices: a whole 4x4x4 slice. The times are simulated.
128 devices in a mesh: fam: 4 (over z), ctx: 32 (over x, y, core).
Axes of the slice: x: 4, y: 4, z: 4, core: 2. Of those that a mesh axis runs over, the one named last changes fastest.
Arguments:
- queries: bfloat16 [4, 16384, 1024], P('fam', 'ctx'), may hold values from -7 to 7
- key_rows: bfloat16 [4, 16384, 1024], P('fam', 'ctx'), may hold values from -4 to 4
- value_rows: bfloat16 [4, 16384, 1024], P('fam', 'ctx'), may hold values from -6 to 6
- cotangent: bfloat16 [4, 16384, 1024], P('fam', 'ctx'), may hold values from -6 to 6
- out_weight: bfloat16 [1024, 1024], replicated, may hold values from -0.1875 to 0.1875
- prot_blocks: int32 [4, 32], P('fam'), may hold values from 1 to 8, 128 in all within a row
- last_fill: int32 [4, 32], P('fam'), may hold values from 1 to 128
- memory_slots: int32 [4, 512], P('fam'), may hold values from 0 to 511
Outputs:
- query_grad: bfloat16 [4, 16384, 1024], P('fam', 'ctx')
- key_grad: bfloat16 [4, 16384, 1024], P('fam', 'ctx')
- value_grad: bfloat16 [4, 16384, 1024], P('fam', 'ctx')
- weight_grad: float32 [1024, 1024], replicated
Inputs may be any that keep to these rules, and one draw needn't show every extreme that they name: `prot_blocks`: each family's protein lengths, in blocks, sum to 128, and the longest has exactly 8 blocks.
All inputs are finite; a program needn't handle non-finite values.
Results may differ from a plain program's by a relative error of at most 0.015.
Values may be sent and summed in bfloat16 or wider, within the bound.
A program may use at most 128 MiB of HBM per device.

v0:
```python
import jax
import jax.numpy as jnp
from jax import lax
from jax.sharding import PartitionSpec as P

HEAD_DIM = 64
W = 512
BLK = 128
NEG_FILL = -1e30


def passed_along(value, axis, steps):
    count = lax.axis_size(axis)
    initial, last = (max(0, -steps), min(count, count - steps))
    return lax.ppermute(value, axis, [(source, source + steps) for source in range(initial, last)])


def protein_tables(prot_blocks, last_fill):
    prot_ends = jnp.cumsum(prot_blocks)
    starts = prot_ends - prot_blocks
    valid_len = (prot_blocks - 1) * BLK + last_fill
    return (prot_ends, starts, valid_len)


def token_info(positions, tables):
    prot_ends, starts, valid_len = tables
    prot_count = prot_ends.shape[0]
    block_ids = jnp.floor_divide(positions, BLK)
    protein = jnp.sum((block_ids[:, None] >= prot_ends[None, :]).astype(jnp.int32), axis=1)
    onehot = protein[:, None] == jnp.arange(prot_count, dtype=jnp.int32)[None, :]
    first_block = jnp.sum(jnp.where(onehot, starts[None, :], 0), axis=1)
    allowed = jnp.sum(jnp.where(onehot, valid_len[None, :], 0), axis=1)
    is_valid = (positions >= 0) & (protein < prot_count) & (positions - first_block * BLK < allowed)
    return (protein, is_valid)


def band_mask(query_pos, query_info, key_pos, key_info):
    return (
        query_info[1][:, None]
        & key_info[1][None, :]
        & (query_info[0][:, None] == key_info[0][None, :])
        & (key_pos[None, :] <= query_pos[:, None])
        & (query_pos[:, None] - key_pos[None, :] < W)
    )


def columns_of(array, column, span):
    return lax.dynamic_slice_in_dim(array, column, span, 1)


def add_into(target, update, row_start, column):
    row_index = jnp.asarray(row_start, jnp.int32)
    current = lax.dynamic_slice(target, (row_index, column), update.shape)
    return lax.dynamic_update_slice(target, current + update, (row_index, column))


def attend(query_blk, grad_blk, key_blk, value_blk, live_mask):
    scale = HEAD_DIM ** (-0.5)
    scores = (
        jnp.einsum("qge,kge->gqk", query_blk, key_blk, preferred_element_type=jnp.float32) * scale
    )
    live = live_mask[None]
    shifted = jnp.where(live, scores, NEG_FILL)
    row_max = jnp.max(shifted, axis=-1, keepdims=True)
    expo = jnp.where(live, jnp.exp(shifted - row_max), 0.0)
    row_sum = jnp.maximum(jnp.sum(expo, axis=-1, keepdims=True), 1.0)
    attn_prob = expo / row_sum
    prob_half = attn_prob.astype(jnp.bfloat16)
    attended = jnp.einsum(
        "gqk,kge->qge", prob_half, value_blk, preferred_element_type=jnp.float32
    ).astype(jnp.bfloat16)
    grad_prob = jnp.einsum("qge,kge->gqk", grad_blk, value_blk, preferred_element_type=jnp.float32)
    row_dot = jnp.sum(attn_prob * grad_prob, axis=-1, keepdims=True)
    grad_score = (attn_prob * (grad_prob - row_dot) * scale).astype(jnp.bfloat16)
    grad_query = jnp.einsum("gqk,kge->qge", grad_score, key_blk, preferred_element_type=jnp.float32)
    grad_key = jnp.einsum("gqk,qge->kge", grad_score, query_blk, preferred_element_type=jnp.float32)
    grad_value = jnp.einsum("gqk,qge->kge", prob_half, grad_blk, preferred_element_type=jnp.float32)
    return (attended, grad_query, grad_key, grad_value, row_max, row_sum, row_dot)


def per_device(
    queries, key_rows, value_rows, cotangent, out_weight, prot_blocks, last_fill, memory_slots
):
    query_loc = queries[0]
    key_loc = key_rows[0]
    value_loc = value_rows[0]
    grad_out = cotangent[0]
    tables = protein_tables(prot_blocks[0], last_fill[0])
    slots = memory_slots[0]
    tokens, width = query_loc.shape
    span = 2 * HEAD_DIM
    pair_count = width // span
    heads_total = width // HEAD_DIM
    ctx_size = lax.axis_size("ctx")
    ctx_index = lax.axis_index("ctx")
    slot_total = slots.shape[0]
    slot_dev = slot_total // ctx_size
    base = ctx_index * tokens
    positions = base + jnp.arange(tokens, dtype=jnp.int32)
    own_info = token_info(positions, tables)
    ext_pos = base - W + jnp.arange(W + tokens, dtype=jnp.int32)
    ext_info = token_info(ext_pos, tables)
    source = jnp.arange(slot_total, dtype=jnp.int32) // slot_dev * tokens + slots
    mem_info = token_info(source, tables)
    own_slots = lax.dynamic_slice_in_dim(slots, ctx_index * slot_dev, slot_dev)
    mem_keys, mem_values = (
        lax.all_gather(key_loc[own_slots], "ctx", axis=0, tiled=True),
        lax.all_gather(value_loc[own_slots], "ctx", axis=0, tiled=True),
    )
    halo_keys, halo_values = passed_along((key_loc, value_loc), "ctx", 1)
    ext_keys = jnp.concatenate([halo_keys, key_loc], axis=0)
    ext_values = jnp.concatenate([halo_values, value_loc], axis=0)
    grad_attn = jnp.einsum(
        "te,de->td", grad_out, out_weight, preferred_element_type=jnp.float32
    ).astype(jnp.bfloat16)
    masks = []
    query_info = (own_info[0], own_info[1])
    key_info = (ext_info[0], ext_info[1])
    band = band_mask(positions, query_info, ext_pos, key_info)
    memory = (
        query_info[1][:, None]
        & mem_info[1][None, :]
        & (mem_info[0][None, :] < query_info[0][:, None])
    )
    masks.append(jnp.concatenate([band, memory], axis=1))

    def pair_step(head_pair, carry):
        (
            query_grad,
            band_kgrad,
            band_vgrad,
            mem_kgrad,
            mem_vgrad,
            attn_rows,
            stat_max,
            stat_sum,
            stat_dot,
        ) = carry
        column = head_pair * span
        query_pair = columns_of(query_loc, column, span).reshape(tokens, 2, HEAD_DIM)
        dout_pair = columns_of(grad_attn, column, span).reshape(tokens, 2, HEAD_DIM)
        key_band = columns_of(ext_keys, column, span).reshape(W + tokens, 2, HEAD_DIM)
        value_band = columns_of(ext_values, column, span).reshape(W + tokens, 2, HEAD_DIM)
        key_memory = columns_of(mem_keys, column, span).reshape(slot_total, 2, HEAD_DIM)
        value_memory = columns_of(mem_values, column, span).reshape(slot_total, 2, HEAD_DIM)
        key_blk = jnp.concatenate([key_band, key_memory], axis=0)
        value_blk = jnp.concatenate([value_band, value_memory], axis=0)
        attended, grad_query, grad_key, grad_value, row_max, row_sum, row_dot = attend(
            query_pair, dout_pair, key_blk, value_blk, masks[0]
        )
        row_index = jnp.asarray(0, jnp.int32)
        query_grad = lax.dynamic_update_slice(
            query_grad, grad_query.reshape(W, span), (row_index, column)
        )
        attn_rows = lax.dynamic_update_slice(
            attn_rows, attended.reshape(W, span), (row_index, column)
        )
        band_kgrad = add_into(band_kgrad, grad_key[: 2 * W].reshape(2 * W, span), 0, column)
        band_vgrad = add_into(band_vgrad, grad_value[: 2 * W].reshape(2 * W, span), 0, column)
        mem_kgrad = add_into(mem_kgrad, grad_key[2 * W :].reshape(slot_total, span), 0, column)
        mem_vgrad = add_into(mem_vgrad, grad_value[2 * W :].reshape(slot_total, span), 0, column)
        stat_col = head_pair * 2
        zero_row = jnp.asarray(0, jnp.int32)
        stat_max = lax.dynamic_update_slice(stat_max, row_max[:, :, 0].T, (zero_row, stat_col))
        stat_sum = lax.dynamic_update_slice(stat_sum, row_sum[:, :, 0].T, (zero_row, stat_col))
        stat_dot = lax.dynamic_update_slice(stat_dot, row_dot[:, :, 0].T, (zero_row, stat_col))
        return (
            query_grad,
            band_kgrad,
            band_vgrad,
            mem_kgrad,
            mem_vgrad,
            attn_rows,
            stat_max,
            stat_sum,
            stat_dot,
        )

    init = (
        jnp.zeros((tokens, width), jnp.float32),
        jnp.zeros((W + tokens, width), jnp.float32),
        jnp.zeros((W + tokens, width), jnp.float32),
        jnp.zeros((slot_total, width), jnp.float32),
        jnp.zeros((slot_total, width), jnp.float32),
        jnp.zeros((tokens, width), jnp.bfloat16),
        jnp.zeros((W, heads_total), jnp.float32),
        jnp.zeros((W, heads_total), jnp.float32),
        jnp.zeros((W, heads_total), jnp.float32),
    )
    (
        query_grad,
        band_kgrad,
        band_vgrad,
        mem_kgrad,
        mem_vgrad,
        attn_rows,
        stat_max,
        stat_sum,
        stat_dot,
    ) = lax.fori_loop(0, pair_count, pair_step, init)
    own_kgrad = band_kgrad[W:]
    own_vgrad = band_vgrad[W:]
    back_kgrad, back_vgrad = (
        passed_along(band_kgrad[:W].astype(jnp.bfloat16), "ctx", -1).astype(jnp.float32),
        passed_along(band_vgrad[:W].astype(jnp.bfloat16), "ctx", -1).astype(jnp.float32),
    )
    own_kgrad = own_kgrad.at[tokens - W :].add(back_kgrad)
    own_vgrad = own_vgrad.at[tokens - W :].add(back_vgrad)
    got_kgrad, got_vgrad = (
        lax.psum_scatter(
            mem_kgrad.astype(jnp.bfloat16), "ctx", scatter_dimension=0, tiled=True
        ).astype(jnp.float32),
        lax.psum_scatter(
            mem_vgrad.astype(jnp.bfloat16), "ctx", scatter_dimension=0, tiled=True
        ).astype(jnp.float32),
    )
    own_kgrad = own_kgrad.at[own_slots].add(got_kgrad)
    own_vgrad = own_vgrad.at[own_slots].add(got_vgrad)
    weight_part = lax.dot_general(
        attn_rows, grad_out, (((0,), (0,)), ((), ())), preferred_element_type=jnp.float32
    )
    weight_total = lax.psum(weight_part, ("fam", "ctx"))
    weight_grad = weight_total * (lax.axis_size("fam") * ctx_size * tokens) ** (-0.5)
    return (
        query_grad.astype(jnp.bfloat16)[None],
        own_kgrad.astype(jnp.bfloat16)[None],
        own_vgrad.astype(jnp.bfloat16)[None],
        weight_grad,
    )


def solution(mesh):
    return jax.shard_map(
        per_device,
        mesh=mesh,
        in_specs=(
            P("fam", "ctx", None),
            P("fam", "ctx", None),
            P("fam", "ctx", None),
            P("fam", "ctx", None),
            P(),
            P("fam", None),
            P("fam", None),
            P("fam", None),
        ),
        out_specs=(P("fam", "ctx", None), P("fam", "ctx", None), P("fam", "ctx", None), P()),
        check_vma=False,
    )
```

profile of v0, /device:TPU:1, one launch (start us, length us, event | category | flops | bytes accessed | tf_op | source)
XLA Modules:
  0.0 967.8 jit_solution(17995845950725439622)
XLA Ops:
  11.3 4.6 collective-permute-start.1
  33.3 6.4 collective-permute-done
  44.0 19.9 %all-gather.7.cloned.1.call-done = bf16[512,1024]{1,0:T(8,128)(2,1)} async-done(((bf16[16,1024]{1,0:T(8,128)(2,1)}), bf16[512,1024]{1,0:T(8,128)(2,1)}) %all-gather.7.cloned.1.call-update) | async-done | bytes 1048592 | tf_op jit(solution)/shard_map/all_gather | solution.py:108
  63.9 44.9 %all-gather.5.cloned.1.call-done = bf16[512,1024]{1,0:T(8,128)(2,1)} async-done(((bf16[16,1024]{1,0:T(8,128)(2,1)}), bf16[512,1024]{1,0:T(8,128)(2,1)}) %all-gather.5.cloned.1.call-update) | async-done | bytes 1048592 | tf_op jit(solution)/shard_map/all_gather | solution.py:107
  118.0 518.4 %while.27 = (s32[]{:T(128)}, bf16[512,1024]{1,0:T(8,128)(2,1)}, f32[1024,1024]{1,0:T(8,128)}, f32[1024,1024]{1,0:T(8,128)}, f32[512,1024]{1,0:T(8,128)}, /*index...) while((s32[]{:T(128)}, bf16[512,1024]{1,0:T(8,128)(2,1)}, ...), condition=%wide.region_14.15_spmd, body=%wide.region_10.14_spmd.sunk | while | flops 1247747584 | bytes 80244984 | solution.py:200
  132.8 7.0 fusion.100
  139.8 4.6 fusion.103
  144.4 13.6 %fusion.101 = bf16[2,64,512]{2,1,0:T(8,128)(2,1)S(1)} fusion(f32[2,512,1536]{2,1,0:T(8,128)} %fusion.99, bf16[512,2,64]{0,2,1:T(8,128)(2,1)S(1)} %bitcast.109, bf16[1024,2,64]{0,2,1:T(8,128)(2,1)S(1)} %bitcast.104, f32[2,512,1536]{2,1,0:T(8,128)} %get-tuple-element.467, f32[2,512]{1,0:T(2,128)S(1)} %broadcast_maximum_fusion.2), kind=kOutput, calls=%fused_computation.16.clone.1 | convolution fusion | flops 213125632 | bytes 13111296 | tf_op jit(solution)/shard_map/while/body/eval_jaxpr/gqk,kge->qge/dot_general | solution.py:75
  157.9 13.2 %fusion.102 = f32[1536,2,64]{0,2,1:T(8,128)S(1)} fusion(bf16[512,2,64]{0,2,1:T(8,128)(2,1)S(1)} %bitcast.107, f32[2,512,1536]{2,1,0:T(8,128)} %fusion.99, f32[2,512,1536]{2,1,0:T(8,128)} %get-tuple-element.467, f32[2,512]{1,0:T(2,128)S(1)} %broadcast_maximum_fusion.2), kind=kOutput, calls=%fused_computation.18.clone.1 | convolution fusion | flops 212339200 | bytes 13504512 | tf_op jit(solution)/shard_map/while/body/eval_jaxpr/gqk,qge->kge/dot_general | solution.py:76
  171.1 4.4 convolution_bitcast_fusion.2
  197.6 7.0 fusion.100
  204.6 4.6 fusion.103
  209.2 13.6 %fusion.101 = bf16[2,64,512]{2,1,0:T(8,128)(2,1)S(1)} fusion(f32[2,512,1536]{2,1,0:T(8,128)} %fusion.99, bf16[512,2,64]{0,2,1:T(8,128)(2,1)S(1)} %bitcast.109, bf16[1024,2,64]{0,2,1:T(8,128)(2,1)S(1)} %bitcast.104, f32[2,512,1536]{2,1,0:T(8,128)} %get-tuple-element.467, f32[2,512]{1,0:T(2,128)S(1)} %broadcast_maximum_fusion.2), kind=kOutput, calls=%fused_computation.16.clone.1 | convolution fusion | flops 213125632 | bytes 13111296 | tf_op jit(solution)/shard_map/while/body/eval_jaxpr/gqk,kge->qge/dot_general | solution.py:75
  222.7 13.2 %fusion.102 = f32[1536,2,64]{0,2,1:T(8,128)S(1)} fusion(bf16[512,2,64]{0,2,1:T(8,128)(2,1)S(1)} %bitcast.107, f32[2,512,1536]{2,1,0:T(8,128)} %fusion.99, f32[2,512,1536]{2,1,0:T(8,128)} %get-tuple-element.467, f32[2,512]{1,0:T(2,128)S(1)} %broadcast_maximum_fusion.2), kind=kOutput, calls=%fused_computation.18.clone.1 | convolution fusion | flops 212339200 | bytes 13504512 | tf_op jit(solution)/shard_map/while/body/eval_jaxpr/gqk,qge->kge/dot_general | solution.py:76
  235.9 4.4 convolution_bitcast_fusion.2
  262.4 7.0 fusion.100
  269.4 4.6 fusion.103
  274.0 13.6 %fusion.101 = bf16[2,64,512]{2,1,0:T(8,128)(2,1)S(1)} fusion(f32[2,512,1536]{2,1,0:T(8,128)} %fusion.99, bf16[512,2,64]{0,2,1:T(8,128)(2,1)S(1)} %bitcast.109, bf16[1024,2,64]{0,2,1:T(8,128)(2,1)S(1)} %bitcast.104, f32[2,512,1536]{2,1,0:T(8,128)} %get-tuple-element.467, f32[2,512]{1,0:T(2,128)S(1)} %broadcast_maximum_fusion.2), kind=kOutput, calls=%fused_computation.16.clone.1 | convolution fusion | flops 213125632 | bytes 13111296 | tf_op jit(solution)/shard_map/while/body/eval_jaxpr/gqk,kge->qge/dot_general | solution.py:75
  287.5 13.2 %fusion.102 = f32[1536,2,64]{0,2,1:T(8,128)S(1)} fusion(bf16[512,2,64]{0,2,1:T(8,128)(2,1)S(1)} %bitcast.107, f32[2,512,1536]{2,1,0:T(8,128)} %fusion.99, f32[2,512,1536]{2,1,0:T(8,128)} %get-tuple-element.467, f32[2,512]{1,0:T(2,128)S(1)} %broadcast_maximum_fusion.2), kind=kOutput, calls=%fused_computation.18.clone.1 | convolution fusion | flops 212339200 | bytes 13504512 | tf_op jit(solution)/shard_map/while/body/eval_jaxpr/gqk,qge->kge/dot_general | solution.py:76
  327.2 7.0 fusion.100
  334.3 4.6 fusion.103
  338.8 13.6 %fusion.101 = bf16[2,64,512]{2,1,0:T(8,128)(2,1)S(1)} fusion(f32[2,512,1536]{2,1,0:T(8,128)} %fusion.99, bf16[512,2,64]{0,2,1:T(8,128)(2,1)S(1)} %bitcast.109, bf16[1024,2,64]{0,2,1:T(8,128)(2,1)S(1)} %bitcast.104, f32[2,512,1536]{2,1,0:T(8,128)} %get-tuple-element.467, f32[2,512]{1,0:T(2,128)S(1)} %broadcast_maximum_fusion.2), kind=kOutput, calls=%fused_computation.16.clone.1 | convolution fusion | flops 213125632 | bytes 13111296 | tf_op jit(solution)/shard_map/while/body/eval_jaxpr/gqk,kge->qge/dot_general | solution.py:75
  352.4 13.2 %fusion.102 = f32[1536,2,64]{0,2,1:T(8,128)S(1)} fusion(bf16[512,2,64]{0,2,1:T(8,128)(2,1)S(1)} %bitcast.107, f32[2,512,1536]{2,1,0:T(8,128)} %fusion.99, f32[2,512,1536]{2,1,0:T(8,128)} %get-tuple-element.467, f32[2,512]{1,0:T(2,128)S(1)} %broadcast_maximum_fusion.2), kind=kOutput, calls=%fused_computation.18.clone.1 | convolution fusion | flops 212339200 | bytes 13504512 | tf_op jit(solution)/shard_map/while/body/eval_jaxpr/gqk,qge->kge/dot_general | solution.py:76
  365.5 4.4 convolution_bitcast_fusion.2
  392.0 7.0 fusion.100
  399.1 4.6 fusion.103
  403.6 13.6 %fusion.101 = bf16[2,64,512]{2,1,0:T(8,128)(2,1)S(1)} fusion(f32[2,512,1536]{2,1,0:T(8,128)} %fusion.99, bf16[512,2,64]{0,2,1:T(8,128)(2,1)S(1)} %bitcast.109, bf16[1024,2,64]{0,2,1:T(8,128)(2,1)S(1)} %bitcast.104, f32[2,512,1536]{2,1,0:T(8,128)} %get-tuple-element.467, f32[2,512]{1,0:T(2,128)S(1)} %broadcast_maximum_fusion.2), kind=kOutput, calls=%fused_computation.16.clone.1 | convolution fusion | flops 213125632 | bytes 13111296 | tf_op jit(solution)/shard_map/while/body/eval_jaxpr/gqk,kge->qge/dot_general | solution.py:75
  417.2 13.2 %fusion.102 = f32[1536,2,64]{0,2,1:T(8,128)S(1)} fusion(bf16[512,2,64]{0,2,1:T(8,128)(2,1)S(1)} %bitcast.107, f32[2,512,1536]{2,1,0:T(8,128)} %fusion.99, f32[2,512,1536]{2,1,0:T(8,128)} %get-tuple-element.467, f32[2,512]{1,0:T(2,128)S(1)} %broadcast_maximum_fusion.2), kind=kOutput, calls=%fused_computation.18.clone.1 | convolution fusion | flops 212339200 | bytes 13504512 | tf_op jit(solution)/shard_map/while/body/eval_jaxpr/gqk,qge->kge/dot_general | solution.py:76
  430.3 4.4 convolution_bitcast_fusion.2
  456.9 7.0 fusion.100
  463.9 4.6 fusion.103
  468.4 13.6 %fusion.101 = bf16[2,64,512]{2,1,0:T(8,128)(2,1)S(1)} fusion(f32[2,512,1536]{2,1,0:T(8,128)} %fusion.99, bf16[512,2,64]{0,2,1:T(8,128)(2,1)S(1)} %bitcast.109, bf16[1024,2,64]{0,2,1:T(8,128)(2,1)S(1)} %bitcast.104, f32[2,512,1536]{2,1,0:T(8,128)} %get-tuple-element.467, f32[2,512]{1,0:T(2,128)S(1)} %broadcast_maximum_fusion.2), kind=kOutput, calls=%fused_computation.16.clone.1 | convolution fusion | flops 213125632 | bytes 13111296 | tf_op jit(solution)/shard_map/while/body/eval_jaxpr/gqk,kge->qge/dot_general | solution.py:75
  482.0 13.2 %fusion.102 = f32[1536,2,64]{0,2,1:T(8,128)S(1)} fusion(bf16[512,2,64]{0,2,1:T(8,128)(2,1)S(1)} %bitcast.107, f32[2,512,1536]{2,1,0:T(8,128)} %fusion.99, f32[2,512,1536]{2,1,0:T(8,128)} %get-tuple-element.467, f32[2,512]{1,0:T(2,128)S(1)} %broadcast_maximum_fusion.2), kind=kOutput, calls=%fused_computation.18.clone.1 | convolution fusion | flops 212339200 | bytes 13504512 | tf_op jit(solution)/shard_map/while/body/eval_jaxpr/gqk,qge->kge/dot_general | solution.py:76
  521.6 7.0 fusion.100
  528.6 4.6 fusion.103
  533.2 13.6 %fusion.101 = bf16[2,64,512]{2,1,0:T(8,128)(2,1)S(1)} fusion(f32[2,512,1536]{2,1,0:T(8,128)} %fusion.99, bf16[512,2,64]{0,2,1:T(8,128)(2,1)S(1)} %bitcast.109, bf16[1024,2,64]{0,2,1:T(8,128)(2,1)S(1)} %bitcast.104, f32[2,512,1536]{2,1,0:T(8,128)} %get-tuple-element.467, f32[2,512]{1,0:T(2,128)S(1)} %broadcast_maximum_fusion.2), kind=kOutput, calls=%fused_computation.16.clone.1 | convolution fusion | flops 213125632 | bytes 13111296 | tf_op jit(solution)/shard_map/while/body/eval_jaxpr/gqk,kge->qge/dot_general | solution.py:75
  546.8 13.2 %fusion.102 = f32[1536,2,64]{0,2,1:T(8,128)S(1)} fusion(bf16[512,2,64]{0,2,1:T(8,128)(2,1)S(1)} %bitcast.107, f32[2,512,1536]{2,1,0:T(8,128)} %fusion.99, f32[2,512,1536]{2,1,0:T(8,128)} %get-tuple-element.467, f32[2,512]{1,0:T(2,128)S(1)} %broadcast_maximum_fusion.2), kind=kOutput, calls=%fused_computation.18.clone.1 | convolution fusion | flops 212339200 | bytes 13504512 | tf_op jit(solution)/shard_map/while/body/eval_jaxpr/gqk,qge->kge/dot_general | solution.py:76
  586.4 7.0 fusion.100
  593.4 4.6 fusion.103
  598.0 13.6 %fusion.101 = bf16[2,64,512]{2,1,0:T(8,128)(2,1)S(1)} fusion(f32[2,512,1536]{2,1,0:T(8,128)} %fusion.99, bf16[512,2,64]{0,2,1:T(8,128)(2,1)S(1)} %bitcast.109, bf16[1024,2,64]{0,2,1:T(8,128)(2,1)S(1)} %bitcast.104, f32[2,512,1536]{2,1,0:T(8,128)} %get-tuple-element.467, f32[2,512]{1,0:T(2,128)S(1)} %broadcast_maximum_fusion.2), kind=kOutput, calls=%fused_computation.16.clone.1 | convolution fusion | flops 213125632 | bytes 13111296 | tf_op jit(solution)/shard_map/while/body/eval_jaxpr/gqk,kge->qge/dot_general | solution.py:75
  611.6 13.2 %fusion.102 = f32[1536,2,64]{0,2,1:T(8,128)S(1)} fusion(bf16[512,2,64]{0,2,1:T(8,128)(2,1)S(1)} %bitcast.107, f32[2,512,1536]{2,1,0:T(8,128)} %fusion.99, f32[2,512,1536]{2,1,0:T(8,128)} %get-tuple-element.467, f32[2,512]{1,0:T(2,128)S(1)} %broadcast_maximum_fusion.2), kind=kOutput, calls=%fused_computation.18.clone.1 | convolution fusion | flops 212339200 | bytes 13504512 | tf_op jit(solution)/shard_map/while/body/eval_jaxpr/gqk,qge->kge/dot_general | solution.py:76
  644.8 4.8 fusion.41
  653.6 5.0 collective-permute-done.3
  660.6 9.2 collective-permute-done.2
  671.4 43.8 %reduce-scatter.5.cloned.1.call-done = bf16[16,1024]{1,0:T(8,128)(2,1)} async-done(((bf16[512,1024]{1,0:T(8,128)(2,1)}), bf16[16,1024]{1,0:T(8,128)(2,1)}) %reduce-scatter.5.cloned.1.call-update) | async-done | bytes 32784 | tf_op jit(solution)/shard_map/reduce_scatter | solution.py:213
  716.9 79.4 %reduce-scatter.3.cloned.1.call-done = bf16[16,1024]{1,0:T(8,128)(2,1)} async-done(((bf16[512,1024]{1,0:T(8,128)(2,1)}), bf16[16,1024]{1,0:T(8,128)(2,1)}) %reduce-scatter.3.cloned.1.call-update) | async-done | bytes 32784 | tf_op jit(solution)/shard_map/reduce_scatter | solution.py:210
  804.2 152.1 %all-reduce.2.cloned.1.call-done = f32[1024,1024]{1,0:T(8,128)} async-done(((f32[1024,1024]{1,0:T(8,128)}), f32[1024,1024]{1,0:T(8,128)}) %all-reduce.2.cloned.1.call-update) | async-done | bytes 4194320 | tf_op jit(solution)/shard_map/psum | solution.py:222
  956.3 5.0 broadcast_multiply_fusion
  (379 shorter events, 253.4 us)
Async XLA Ops:
  7.2 22.5 %copy-start = (bf16[1024,1024]{1,0:T(8,128)(2,1)S(1)}, bf16[1024,1024]{1,0:T(8,128)(2,1)}, u32[]{:S(2)}) copy-start(bf16[1024,1024]{1,0:T(8,128)(2,1)} %param.22) | copy-start | bytes 6291460
  7.2 56.7 %all-gather.7.cloned.1.call-start = ((), (), s32[]{:S(2)}) async-start(), calls=%async_computation.6 | async-start | bytes 1081344 | tf_op jit(solution)/shard_map/all_gather | solution.py:108
  8.1 0.5 copy-start.6
  11.2 97.5 %all-gather.5.cloned.1.call-start = ((), (), s32[]{:S(2)}) async-start(), calls=%async_computation.5 | async-start | bytes 1081344 | tf_op jit(solution)/shard_map/all_gather | solution.py:107
  11.3 31.3 %collective-permute-start.1 = (bf16[512,1024]{1,0:T(8,128)(2,1)}, bf16[512,1024]{1,0:T(8,128)(2,1)S(1)}, u32[]{:S(2)}, u32[]{:S(2)}) collective-permute-start(bf16[512,1024]{1,0:T(8,128)(2,1)} %bitcast.115), channel_id=1, source_target_pairs={{0,1},{1,2},{2,3},{3,4},{4,5},{5,6},{6,7},{7,8},{8,9},{9,10},{10,1... | collective-permute-start | bytes 3145736 | tf_op jit(solution)/shard_map/ppermute | solution.py:15
  15.9 23.8 %collective-permute-start = (bf16[512,1024]{1,0:T(8,128)(2,1)}, bf16[512,1024]{1,0:T(8,128)(2,1)}, u32[]{:S(2)}, u32[]{:S(2)}) collective-permute-start(bf16[512,1024]{1,0:T(8,128)(2,1)} %bitcast.111), channel_id=1, source_target_pairs={{0,1},{1,2},{2,3},{3,4},{4,5},{5,6},{6,7},{7,8},{8,9},{9,10},{10,1... | collective-permute-start | bytes 3145736 | tf_op jit(solution)/shard_map/ppermute | solution.py:15
  20.4 694.8 %reduce-scatter.5.cloned.1.call-start = ((), (), s32[]{:S(2)}) async-start(), calls=%async_computation.3 | async-start | bytes 1081344 | tf_op jit(solution)/shard_map/reduce_scatter | solution.py:213
  29.7 10.0 %copy-start.4 = (bf16[1,512,1024]{2,1,0:T(8,128)(2,1)S(1)}, bf16[1,512,1024]{2,1,0:T(8,128)(2,1)}, u32[]{:S(2)}) copy-start(bf16[1,512,1024]{2,1,0:T(8,128)(2,1)} %param.19) | copy-start | bytes 3145732
  33.3 9.3 copy-start.5
  636.4 3.1 copy-start.3
  639.4 156.9 %reduce-scatter.3.cloned.1.call-start = ((), (), s32[]{:S(2)}) async-start(), calls=%async_computation.2 | async-start | bytes 1081344 | tf_op jit(solution)/shard_map/reduce_scatter | solution.py:210
  640.7 315.6 %all-reduce.2.cloned.1.call-start = ((), (), s32[]{:S(2)}) async-start(), calls=%async_computation.4 | async-start | bytes 8388608 | tf_op jit(solution)/shard_map/psum | solution.py:222
  642.5 16.1 %collective-permute-start.3 = (bf16[512,1024]{1,0:T(8,128)(2,1)S(1)}, bf16[512,1024]{1,0:T(8,128)(2,1)S(1)}, u32[]{:S(2)}, u32[]{:S(2)}) collective-permute-start(bf16[512,1024]{1,0:T(8,128)(2,1)S(1)} %slice.88), channel_id=1, source_target_pairs={{1,0},{2,1},{3,2},{4,3},{5,4},{6,5},{7,6},{8,7},{9,8},{10,9},{11,1... | collective-permute-start | bytes 3145736 | tf_op jit(solution)/shard_map/ppermute | solution.py:15
  649.6 20.2 %copy-start.2 = (f32[1024,1024]{1,0:T(8,128)S(1)}, f32[1024,1024]{1,0:T(8,128)}, u32[]{:S(2)}) copy-start(f32[1024,1024]{1,0:T(8,128)} %get-tuple-element.279) | copy-start | bytes 12582916
  651.6 18.3 %collective-permute-start.2 = (bf16[512,1024]{1,0:T(8,128)(2,1)S(1)}, bf16[512,1024]{1,0:T(8,128)(2,1)S(1)}, u32[]{:S(2)}, u32[]{:S(2)}) collective-permute-start(bf16[512,1024]{1,0:T(8,128)(2,1)S(1)} %slice.89), channel_id=1, source_target_pairs={{1,0},{2,1},{3,2},{4,3},{5,4},{6,5},{7,6},{8,7},{9,8},{10,9},{11,1... | collective-permute-start | bytes 3145736 | tf_op jit(solution)/shard_map/ppermute | solution.py:15
  801.3 160.0 %copy-start.1 = (bf16[1024,1024]{1,0:T(8,128)(2,1)S(1)}, bf16[1024,1024]{1,0:T(8,128)(2,1)}, u32[]{:S(2)}) copy-start(bf16[1024,1024]{1,0:T(8,128)(2,1)} %param.22) | copy-start | bytes 6291460
Sparse Core Ops, SparseCore 0:
  11.4 52.4 all-gather.6
  66.7 41.9 all-gather.4
  639.6 75.6 reduce-scatter.4
  719.5 76.7 reduce-scatter.2
  801.1 155.0 all-reduce.1
where the time goes:
time: 972 us; the launch traced here: 968 us
  matrix products  379 us (39%)
  waiting for transfers between devices  361 us (37%)
  local copies, waits for them, and re-layouts  166 us (17%)
  other arithmetic  35.4 us (4%)
  between operations  13.9 us (1%)
  starting transfers between devices  11.1 us (1%)
    psum x1, waiting for transfers between devices, per_device(): weight_total = lax.psum(weight_part, ('fam', 'ctx'))  152 us
    dot_general x8, matrix products, attend(): jnp.einsum('gqk,kge->qge', grad_score, key_blk, preferred_element_type=jn...  108 us
    dot_general x8, matrix products, attend(): jnp.einsum('gqk,qge->kge', grad_score, query_blk, preferred_element_type=...  105 us
    reduce_scatter x1, waiting for transfers between devices, per_device(): lax.psum_scatter(mem_kgrad.astype(jnp.bfloat16), 'ctx', scatter_dimension...  79.4 us
    sub x8, matrix products, attend(): expo = jnp.where(live, jnp.exp(shifted - row_max), 0.0)  56 us
    dynamic_slice x88, local copies, waits for them, and re-layouts, columns_of(): return lax.dynamic_slice_in_dim(array, column, span, 1)  50 us
    all_gather x1, waiting for transfers between devices, per_device(): lax.all_gather(key_loc[own_slots], 'ctx', axis=0, tiled=True)  44.9 us
    reduce_scatter x1, waiting for transfers between devices, per_device(): lax.psum_scatter(mem_vgrad.astype(jnp.bfloat16), 'ctx', scatter_dimension...  43.8 us
  transfers between devices with their start and end apart: 9, of which 8 were waited for; matrix products, arithmetic and copies ran while one was open for 4% of the time, Pallas kernels for 0%

commit v1 on v0

--- a/solution.py
+++ b/solution.py
@@ -104,7 +104,10 @@
     mem_info = token_info(source, tables)
     own_slots = lax.dynamic_slice_in_dim(slots, ctx_index * slot_dev, slot_dev)
     mem_keys, mem_values = (
-        lax.all_gather(key_loc[own_slots], "ctx", axis=0, tiled=True),
+        jnp.concatenate(
+            lax.all_to_all(jnp.stack([key_loc[own_slots]] * lax.axis_size("ctx")), "ctx", 0, 0),
+            axis=0,
+        ),
         lax.all_gather(value_loc[own_slots], "ctx", axis=0, tiled=True),
     )
     halo_keys, halo_values = passed_along((key_loc, value_loc), "ctx", 1)

time: 972 us -> 938 us (0.965)
  waiting for transfers between devices: 361 us -> 315 us
    all_gather x1 -> x0, waiting for transfers between devices: 44.9 us -> none  [per_device(): lax.all_gather(key_loc[own_slots], 'ctx', axis=0, tiled=True)]
  transfers between devices with their start and end apart: 9 -> 9, of which waited for: 8 -> 8; matrix products, arithmetic and copies ran while one was open for 4% -> 5% of each run, Pallas kernels for 0% -> 0%
where the time goes in v1:
time: 938 us; the launch traced here: 933 us
  matrix products  379 us (40%)
  waiting for transfers between devices  315 us (34%)
  local copies, waits for them, and re-layouts  167 us (18%)
  other arithmetic  37.6 us (4%)
  starting transfers between devices  18.5 us (2%)
  between operations  14 us (1%)
    psum x1, waiting for transfers between devices, per_device(): weight_total = lax.psum(weight_part, ('fam', 'ctx'))  152 us
    dot_general x8, matrix products, attend(): jnp.einsum('gqk,kge->qge', grad_score, key_blk, preferred_element_type=jn...  108 us
    dot_general x8, matrix products, attend(): jnp.einsum('gqk,qge->kge', grad_score, query_blk, preferred_element_type=...  105 us
    reduce_scatter x1, waiting for transfers between devices, per_device(): lax.psum_scatter(mem_kgrad.astype(jnp.bfloat16), 'ctx', scatter_dimension...  79.5 us
    sub x8, matrix products, attend(): expo = jnp.where(live, jnp.exp(shifted - row_max), 0.0)  56 us
    dynamic_slice x88, local copies, waits for them, and re-layouts, columns_of(): return lax.dynamic_slice_in_dim(array, column, span, 1)  51 us
    reduce_scatter x1, waiting for transfers between devices, per_device(): lax.psum_scatter(mem_vgrad.astype(jnp.bfloat16), 'ctx', scatter_dimension...  43.7 us
    dynamic_slice x64, local copies, waits for them, and re-layouts, add_into(): current = lax.dynamic_slice(target, (row_index, column), update.shape)  38.1 us
  transfers between devices with their start and end apart: 9, of which 8 were waited for; matrix products, arithmetic and copies ran while one was open for 5% of the time, Pallas kernels for 0%

profile of v1, /device:TPU:1, one launch (start us, length us, event | category | flops | bytes accessed | tf_op | source)
XLA Modules:
  0.0 933.3 jit_solution(17905807958382159702)
XLA Ops:
  7.2 4.7 collective-permute-start.1
  20.3 7.3 all-to-all-start
  52.5 20.4 %all-gather.3.cloned.1.call-done = bf16[512,1024]{1,0:T(8,128)(2,1)} async-done(((bf16[16,1024]{1,0:T(8,128)(2,1)}), bf16[512,1024]{1,0:T(8,128)(2,1)}) %all-gather.3.cloned.1.call-update) | async-done | bytes 1048592 | tf_op jit(solution)/shard_map/all_gather | solution.py:111
  82.1 519.6 %while.27 = (s32[]{:T(128)}, bf16[512,1024]{1,0:T(8,128)(2,1)}, f32[1024,1024]{1,0:T(8,128)}, f32[1024,1024]{1,0:T(8,128)}, f32[512,1024]{1,0:T(8,128)}, /*index...) while((s32[]{:T(128)}, bf16[512,1024]{1,0:T(8,128)(2,1)}, ...), condition=%wide.region_14.15_spmd, body=%wide.region_10.14_spmd.sunk | while | flops 1247747584 | bytes 88633648 | solution.py:203
  97.1 7.0 fusion.100
  104.1 4.6 fusion.103
  108.6 13.6 %fusion.101 = bf16[2,64,512]{2,1,0:T(8,128)(2,1)S(1)} fusion(f32[2,512,1536]{2,1,0:T(8,128)} %fusion.99, bf16[512,2,64]{0,2,1:T(8,128)(2,1)S(1)} %bitcast.110, bf16[1024,2,64]{0,2,1:T(8,128)(2,1)S(1)} %bitcast.105, f32[2,512,1536]{2,1,0:T(8,128)} %get-tuple-element.467, f32[2,512]{1,0:T(2,128)S(1)} %broadcast_maximum_fusion.2), kind=kOutput, calls=%fused_computation.16.clone.1 | convolution fusion | flops 213125632 | bytes 13111296 | tf_op jit(solution)/shard_map/while/body/eval_jaxpr/gqk,kge->qge/dot_general | solution.py:75
  122.2 13.2 %fusion.102 = f32[1536,2,64]{0,2,1:T(8,128)S(1)} fusion(bf16[512,2,64]{0,2,1:T(8,128)(2,1)S(1)} %bitcast.108, f32[2,512,1536]{2,1,0:T(8,128)} %fusion.99, f32[2,512,1536]{2,1,0:T(8,128)} %get-tuple-element.467, f32[2,512]{1,0:T(2,128)S(1)} %broadcast_maximum_fusion.2), kind=kOutput, calls=%fused_computation.18.clone.1 | convolution fusion | flops 212339200 | bytes 13504512 | tf_op jit(solution)/shard_map/while/body/eval_jaxpr/gqk,qge->kge/dot_general | solution.py:76
  135.4 4.4 convolution_bitcast_fusion.2
  162.0 7.0 fusion.100
  169.0 4.6 fusion.103
  173.6 13.6 %fusion.101 = bf16[2,64,512]{2,1,0:T(8,128)(2,1)S(1)} fusion(f32[2,512,1536]{2,1,0:T(8,128)} %fusion.99, bf16[512,2,64]{0,2,1:T(8,128)(2,1)S(1)} %bitcast.110, bf16[1024,2,64]{0,2,1:T(8,128)(2,1)S(1)} %bitcast.105, f32[2,512,1536]{2,1,0:T(8,128)} %get-tuple-element.467, f32[2,512]{1,0:T(2,128)S(1)} %broadcast_maximum_fusion.2), kind=kOutput, calls=%fused_computation.16.clone.1 | convolution fusion | flops 213125632 | bytes 13111296 | tf_op jit(solution)/shard_map/while/body/eval_jaxpr/gqk,kge->qge/dot_general | solution.py:75
  187.2 13.2 %fusion.102 = f32[1536,2,64]{0,2,1:T(8,128)S(1)} fusion(bf16[512,2,64]{0,2,1:T(8,128)(2,1)S(1)} %bitcast.108, f32[2,512,1536]{2,1,0:T(8,128)} %fusion.99, f32[2,512,1536]{2,1,0:T(8,128)} %get-tuple-element.467, f32[2,512]{1,0:T(2,128)S(1)} %broadcast_maximum_fusion.2), kind=kOutput, calls=%fused_computation.18.clone.1 | convolution fusion | flops 212339200 | bytes 13504512 | tf_op jit(solution)/shard_map/while/body/eval_jaxpr/gqk,qge->kge/dot_general | solution.py:76
  200.3 4.4 convolution_bitcast_fusion.2
  227.0 7.0 fusion.100
  234.0 4.6 fusion.103
  238.6 13.6 %fusion.101 = bf16[2,64,512]{2,1,0:T(8,128)(2,1)S(1)} fusion(f32[2,512,1536]{2,1,0:T(8,128)} %fusion.99, bf16[512,2,64]{0,2,1:T(8,128)(2,1)S(1)} %bitcast.110, bf16[1024,2,64]{0,2,1:T(8,128)(2,1)S(1)} %bitcast.105, f32[2,512,1536]{2,1,0:T(8,128)} %get-tuple-element.467, f32[2,512]{1,0:T(2,128)S(1)} %broadcast_maximum_fusion.2), kind=kOutput, calls=%fused_computation.16.clone.1 | convolution fusion | flops 213125632 | bytes 13111296 | tf_op jit(solution)/shard_map/while/body/eval_jaxpr/gqk,kge->qge/dot_general | solution.py:75
  252.1 13.2 %fusion.102 = f32[1536,2,64]{0,2,1:T(8,128)S(1)} fusion(bf16[512,2,64]{0,2,1:T(8,128)(2,1)S(1)} %bitcast.108, f32[2,512,1536]{2,1,0:T(8,128)} %fusion.99, f32[2,512,1536]{2,1,0:T(8,128)} %get-tuple-element.467, f32[2,512]{1,0:T(2,128)S(1)} %broadcast_maximum_fusion.2), kind=kOutput, calls=%fused_computation.18.clone.1 | convolution fusion | flops 212339200 | bytes 13504512 | tf_op jit(solution)/shard_map/while/body/eval_jaxpr/gqk,qge->kge/dot_general | solution.py:76
  265.3 4.4 convolution_bitcast_fusion.2
  292.0 7.0 fusion.100
  299.0 4.6 fusion.103
  303.5 13.6 %fusion.101 = bf16[2,64,512]{2,1,0:T(8,128)(2,1)S(1)} fusion(f32[2,512,1536]{2,1,0:T(8,128)} %fusion.99, bf16[512,2,64]{0,2,1:T(8,128)(2,1)S(1)} %bitcast.110, bf16[1024,2,64]{0,2,1:T(8,128)(2,1)S(1)} %bitcast.105, f32[2,512,1536]{2,1,0:T(8,128)} %get-tuple-element.467, f32[2,512]{1,0:T(2,128)S(1)} %broadcast_maximum_fusion.2), kind=kOutput, calls=%fused_computation.16.clone.1 | convolution fusion | flops 213125632 | bytes 13111296 | tf_op jit(solution)/shard_map/while/body/eval_jaxpr/gqk,kge->qge/dot_general | solution.py:75
  317.1 13.2 %fusion.102 = f32[1536,2,64]{0,2,1:T(8,128)S(1)} fusion(bf16[512,2,64]{0,2,1:T(8,128)(2,1)S(1)} %bitcast.108, f32[2,512,1536]{2,1,0:T(8,128)} %fusion.99, f32[2,512,1536]{2,1,0:T(8,128)} %get-tuple-element.467, f32[2,512]{1,0:T(2,128)S(1)} %broadcast_maximum_fusion.2), kind=kOutput, calls=%fused_computation.18.clone.1 | convolution fusion | flops 212339200 | bytes 13504512 | tf_op jit(solution)/shard_map/while/body/eval_jaxpr/gqk,qge->kge/dot_general | solution.py:76
  330.3 4.4 convolution_bitcast_fusion.2
  356.9 7.0 fusion.100
  363.9 4.6 fusion.103
  368.5 13.6 %fusion.101 = bf16[2,64,512]{2,1,0:T(8,128)(2,1)S(1)} fusion(f32[2,512,1536]{2,1,0:T(8,128)} %fusion.99, bf16[512,2,64]{0,2,1:T(8,128)(2,1)S(1)} %bitcast.110, bf16[1024,2,64]{0,2,1:T(8,128)(2,1)S(1)} %bitcast.105, f32[2,512,1536]{2,1,0:T(8,128)} %get-tuple-element.467, f32[2,512]{1,0:T(2,128)S(1)} %broadcast_maximum_fusion.2), kind=kOutput, calls=%fused_computation.16.clone.1 | convolution fusion | flops 213125632 | bytes 13111296 | tf_op jit(solution)/shard_map/while/body/eval_jaxpr/gqk,kge->qge/dot_general | solution.py:75
  382.0 13.2 %fusion.102 = f32[1536,2,64]{0,2,1:T(8,128)S(1)} fusion(bf16[512,2,64]{0,2,1:T(8,128)(2,1)S(1)} %bitcast.108, f32[2,512,1536]{2,1,0:T(8,128)} %fusion.99, f32[2,512,1536]{2,1,0:T(8,128)} %get-tuple-element.467, f32[2,512]{1,0:T(2,128)S(1)} %broadcast_maximum_fusion.2), kind=kOutput, calls=%fused_computation.18.clone.1 | convolution fusion | flops 212339200 | bytes 13504512 | tf_op jit(solution)/shard_map/while/body/eval_jaxpr/gqk,qge->kge/dot_general | solution.py:76
  395.2 4.4 convolution_bitcast_fusion.2
  421.9 7.0 fusion.100
  428.9 4.6 fusion.103
  433.4 13.6 %fusion.101 = bf16[2,64,512]{2,1,0:T(8,128)(2,1)S(1)} fusion(f32[2,512,1536]{2,1,0:T(8,128)} %fusion.99, bf16[512,2,64]{0,2,1:T(8,128)(2,1)S(1)} %bitcast.110, bf16[1024,2,64]{0,2,1:T(8,128)(2,1)S(1)} %bitcast.105, f32[2,512,1536]{2,1,0:T(8,128)} %get-tuple-element.467, f32[2,512]{1,0:T(2,128)S(1)} %broadcast_maximum_fusion.2), kind=kOutput, calls=%fused_computation.16.clone.1 | convolution fusion | flops 213125632 | bytes 13111296 | tf_op jit(solution)/shard_map/while/body/eval_jaxpr/gqk,kge->qge/dot_general | solution.py:75
  447.0 13.2 %fusion.102 = f32[1536,2,64]{0,2,1:T(8,128)S(1)} fusion(bf16[512,2,64]{0,2,1:T(8,128)(2,1)S(1)} %bitcast.108, f32[2,512,1536]{2,1,0:T(8,128)} %fusion.99, f32[2,512,1536]{2,1,0:T(8,128)} %get-tuple-element.467, f32[2,512]{1,0:T(2,128)S(1)} %broadcast_maximum_fusion.2), kind=kOutput, calls=%fused_computation.18.clone.1 | convolution fusion | flops 212339200 | bytes 13504512 | tf_op jit(solution)/shard_map/while/body/eval_jaxpr/gqk,qge->kge/dot_general | solution.py:76
  486.8 7.0 fusion.100
  493.8 4.6 fusion.103
  498.3 13.6 %fusion.101 = bf16[2,64,512]{2,1,0:T(8,128)(2,1)S(1)} fusion(f32[2,512,1536]{2,1,0:T(8,128)} %fusion.99, bf16[512,2,64]{0,2,1:T(8,128)(2,1)S(1)} %bitcast.110, bf16[1024,2,64]{0,2,1:T(8,128)(2,1)S(1)} %bitcast.105, f32[2,512,1536]{2,1,0:T(8,128)} %get-tuple-element.467, f32[2,512]{1,0:T(2,128)S(1)} %broadcast_maximum_fusion.2), kind=kOutput, calls=%fused_computation.16.clone.1 | convolution fusion | flops 213125632 | bytes 13111296 | tf_op jit(solution)/shard_map/while/body/eval_jaxpr/gqk,kge->qge/dot_general | solution.py:75
  511.9 13.2 %fusion.102 = f32[1536,2,64]{0,2,1:T(8,128)S(1)} fusion(bf16[512,2,64]{0,2,1:T(8,128)(2,1)S(1)} %bitcast.108, f32[2,512,1536]{2,1,0:T(8,128)} %fusion.99, f32[2,512,1536]{2,1,0:T(8,128)} %get-tuple-element.467, f32[2,512]{1,0:T(2,128)S(1)} %broadcast_maximum_fusion.2), kind=kOutput, calls=%fused_computation.18.clone.1 | convolution fusion | flops 212339200 | bytes 13504512 | tf_op jit(solution)/shard_map/while/body/eval_jaxpr/gqk,qge->kge/dot_general | solution.py:76
  551.7 7.0 fusion.100
  558.7 4.6 fusion.103
  563.3 13.6 %fusion.101 = bf16[2,64,512]{2,1,0:T(8,128)(2,1)S(1)} fusion(f32[2,512,1536]{2,1,0:T(8,128)} %fusion.99, bf16[512,2,64]{0,2,1:T(8,128)(2,1)S(1)} %bitcast.110, bf16[1024,2,64]{0,2,1:T(8,128)(2,1)S(1)} %bitcast.105, f32[2,512,1536]{2,1,0:T(8,128)} %get-tuple-element.467, f32[2,512]{1,0:T(2,128)S(1)} %broadcast_maximum_fusion.2), kind=kOutput, calls=%fused_computation.16.clone.1 | convolution fusion | flops 213125632 | bytes 13111296 | tf_op jit(solution)/shard_map/while/body/eval_jaxpr/gqk,kge->qge/dot_general | solution.py:75
  576.8 13.2 %fusion.102 = f32[1536,2,64]{0,2,1:T(8,128)S(1)} fusion(bf16[512,2,64]{0,2,1:T(8,128)(2,1)S(1)} %bitcast.108, f32[2,512,1536]{2,1,0:T(8,128)} %fusion.99, f32[2,512,1536]{2,1,0:T(8,128)} %get-tuple-element.467, f32[2,512]{1,0:T(2,128)S(1)} %broadcast_maximum_fusion.2), kind=kOutput, calls=%fused_computation.18.clone.1 | convolution fusion | flops 212339200 | bytes 13504512 | tf_op jit(solution)/shard_map/while/body/eval_jaxpr/gqk,qge->kge/dot_general | solution.py:76
  610.1 4.8 fusion.41
  618.9 5.0 collective-permute-done.3
  625.9 9.2 collective-permute-done.2
  636.7 43.7 %reduce-scatter.5.cloned.1.call-done = bf16[16,1024]{1,0:T(8,128)(2,1)} async-done(((bf16[512,1024]{1,0:T(8,128)(2,1)}), bf16[16,1024]{1,0:T(8,128)(2,1)}) %reduce-scatter.5.cloned.1.call-update) | async-done | bytes 32784 | tf_op jit(solution)/shard_map/reduce_scatter | solution.py:216
  682.2 79.5 %reduce-scatter.3.cloned.1.call-done = bf16[16,1024]{1,0:T(8,128)(2,1)} async-done(((bf16[512,1024]{1,0:T(8,128)(2,1)}), bf16[16,1024]{1,0:T(8,128)(2,1)}) %reduce-scatter.3.cloned.1.call-update) | async-done | bytes 32784 | tf_op jit(solution)/shard_map/reduce_scatter | solution.py:213
  769.6 152.1 %all-reduce.2.cloned.1.call-done = f32[1024,1024]{1,0:T(8,128)} async-done(((f32[1024,1024]{1,0:T(8,128)}), f32[1024,1024]{1,0:T(8,128)}) %all-reduce.2.cloned.1.call-update) | async-done | bytes 4194320 | tf_op jit(solution)/shard_map/psum | solution.py:225
  921.7 5.0 broadcast_multiply_fusion
  (413 shorter events, 257.5 us)
Async XLA Ops:
  7.2 30.8 %copy-start = (bf16[1024,1024]{1,0:T(8,128)(2,1)S(1)}, bf16[1024,1024]{1,0:T(8,128)(2,1)}, u32[]{:S(2)}) copy-start(bf16[1024,1024]{1,0:T(8,128)(2,1)} %param.22) | copy-start | bytes 6291460
  7.2 25.1 %copy-start.8 = (s32[1,512]{1,0:T(1,128)S(1)}, s32[1,512]{1,0:T(1,128)}, u32[]{:S(2)}) copy-start(s32[1,512]{1,0:T(1,128)} %param.25) | copy-start | bytes 6148
  7.2 65.7 %all-gather.3.cloned.1.call-start = ((), (), s32[]{:S(2)}) async-start(), calls=%async_computation.6 | async-start | bytes 1081344 | tf_op jit(solution)/shard_map/all_gather | solution.py:111
  7.2 41.2 %collective-permute-start.1 = (bf16[512,1024]{1,0:T(8,128)(2,1)}, bf16[512,1024]{1,0:T(8,128)(2,1)}, u32[]{:S(2)}, u32[]{:S(2)}) collective-permute-start(bf16[512,1024]{1,0:T(8,128)(2,1)} %bitcast.116), channel_id=1, source_target_pairs={{0,1},{1,2},{2,3},{3,4},{4,5},{5,6},{6,7},{7,8},{8,9},{9,10},{10,1... | collective-permute-start | bytes 3145736 | tf_op jit(solution)/shard_map/ppermute | solution.py:15
  12.7 7.6 copy-start.9
  15.3 30.3 %collective-permute-start = (bf16[512,1024]{1,0:T(8,128)(2,1)}, bf16[512,1024]{1,0:T(8,128)(2,1)}, u32[]{:S(2)}, u32[]{:S(2)}) collective-permute-start(bf16[512,1024]{1,0:T(8,128)(2,1)} %bitcast.113), channel_id=1, source_target_pairs={{0,1},{1,2},{2,3},{3,4},{4,5},{5,6},{6,7},{7,8},{8,9},{9,10},{10,1... | collective-permute-start | bytes 3145736 | tf_op jit(solution)/shard_map/ppermute | solution.py:15
  20.3 32.1 %all-to-all-start = ((bf16[32,16,1024]{2,1,0:T(8,128)(2,1)}), bf16[32,16,1024]{2,1,0:T(8,128)(2,1)S(1)}, u32[]{:S(2)}, u32[]{:S(2)}) async-start(bf16[32,16,1024]{2,1,0:T(8,128)(2,1)} %stack.2), calls=%async_computation | async-start | bytes 2097152 | tf_op jit(solution)/shard_map/all_to_all | solution.py:108
  27.6 652.9 %reduce-scatter.5.cloned.1.call-start = ((), (), s32[]{:S(2)}) async-start(), calls=%async_computation.4 | async-start | bytes 1081344 | tf_op jit(solution)/shard_map/reduce_scatter | solution.py:216
  38.0 7.6 copy-start.6
  41.5 6.9 copy-start.7
  82.1 2.2 copy-start.4
  142.5 4.6 copy-start.5
  147.1 2.2 copy-start.4
  207.4 4.6 copy-start.5
  212.1 2.2 copy-start.4
  272.4 4.6 copy-start.5
  277.0 2.2 copy-start.4
  337.4 4.6 copy-start.5
  342.0 2.2 copy-start.4
  402.3 4.6 copy-start.5
  406.9 2.2 copy-start.4
  467.3 4.6 copy-start.5
  471.9 2.2 copy-start.4
  532.2 4.6 copy-start.5
  536.8 2.2 copy-start.4
  597.1 4.6 copy-start.5
  601.7 3.1 copy-start.3
  604.7 157.0 %reduce-scatter.3.cloned.1.call-start = ((), (), s32[]{:S(2)}) async-start(), calls=%async_computation.3 | async-start | bytes 1081344 | tf_op jit(solution)/shard_map/reduce_scatter | solution.py:213
  606.0 315.7 %all-reduce.2.cloned.1.call-start = ((), (), s32[]{:S(2)}) async-start(), calls=%async_computation.5 | async-start | bytes 8388608 | tf_op jit(solution)/shard_map/psum | solution.py:225
  607.8 16.1 %collective-permute-start.3 = (bf16[512,1024]{1,0:T(8,128)(2,1)S(1)}, bf16[512,1024]{1,0:T(8,128)(2,1)S(1)}, u32[]{:S(2)}, u32[]{:S(2)}) collective-permute-start(bf16[512,1024]{1,0:T(8,128)(2,1)S(1)} %slice.88), channel_id=1, source_target_pairs={{1,0},{2,1},{3,2},{4,3},{5,4},{6,5},{7,6},{8,7},{9,8},{10,9},{11,1... | collective-permute-start | bytes 3145736 | tf_op jit(solution)/shard_map/ppermute | solution.py:15
  614.9 20.2 %copy-start.2 = (f32[1024,1024]{1,0:T(8,128)S(1)}, f32[1024,1024]{1,0:T(8,128)}, u32[]{:S(2)}) copy-start(f32[1024,1024]{1,0:T(8,128)} %get-tuple-element.279) | copy-start | bytes 12582916
  616.9 18.3 %collective-permute-start.2 = (bf16[512,1024]{1,0:T(8,128)(2,1)S(1)}, bf16[512,1024]{1,0:T(8,128)(2,1)S(1)}, u32[]{:S(2)}, u32[]{:S(2)}) collective-permute-start(bf16[512,1024]{1,0:T(8,128)(2,1)S(1)} %slice.89), channel_id=1, source_target_pairs={{1,0},{2,1},{3,2},{4,3},{5,4},{6,5},{7,6},{8,7},{9,8},{10,9},{11,1... | collective-permute-start | bytes 3145736 | tf_op jit(solution)/shard_map/ppermute | solution.py:15
  766.7 160.0 %copy-start.1 = (bf16[1024,1024]{1,0:T(8,128)(2,1)S(1)}, bf16[1024,1024]{1,0:T(8,128)(2,1)}, u32[]{:S(2)}) copy-start(bf16[1024,1024]{1,0:T(8,128)(2,1)} %param.22) | copy-start | bytes 6291460
Sparse Core Ops, SparseCore 0:
  15.4 57.4 all-gather.2
  604.9 75.5 reduce-scatter.4
  685.0 76.7 reduce-scatter.2
  766.6 155.0 all-reduce.1
